TPU v7x, 512 devices: a whole 4x4x16 slice. The times are simulated.
512 devices in a mesh: outer: 8 (over z_hi, core), inner: 16 (over x, y), head: 4 (over z_lo).
Axes of the slice: x: 4, y: 4, z: 16 (z_hi: 4, z_lo: 4; z = z_hi * 4 + z_lo), core: 2. Of those that a mesh axis runs over, the one named last changes fastest.
Arguments:
- queries: bfloat16 [8192, 2560], P(('outer', 'inner'), 'head'), may hold values from -5 to 5
- keys: bfloat16 [8192, 2560], P(('outer', 'inner'), 'head'), may hold values from -5 to 5
- values: bfloat16 [8192, 2560], P(('outer', 'inner'), 'head'), may hold values from -6 to 6
- slot_blocks: int32 [256], replicated, may hold values from 0 to 255, as said below
- doc_blocks: int32 [4], replicated, may hold values from 1 to 128, 256 in all
Outputs:
- attended: bfloat16 [8192, 2560], P(('outer', 'inner'), 'head')
Inputs may be any that keep to these rules, and one draw needn't show every extreme that they name: `slot_blocks`: slots 2 j and 2 j + 1 hold blocks i and 255 - i for some i below 128; every block stands in one slot.
All inputs are finite; a program needn't handle non-finite values.
Results may differ from a plain program's by a relative error of at most 0.008.
Values may be sent and summed in bfloat16 or wider, within the bound.
A program may use at most 128 MiB of HBM per device.

v0:
```python
import functools
import math

import jax
import jax.numpy as jnp
from jax import lax
from jax.experimental import pallas as pl
from jax.experimental.pallas import tpu as pltpu
from jax.sharding import PartitionSpec as P

D = 128
BLK = 32
R = 64
NX = 4
NZ = 2
NC = 2
NQ = NX * NZ * R
QT = NX * R
KT = NC * NX * BLK
NK = NC * NZ * NX * R
STAT = 16
SCALE2 = D ** (-0.5) * math.log2(math.e)
HIDE = -1e30
FLOOR = -1e29
MESH = pl.DeviceIdType.MESH
F32 = jnp.float32
BF16 = jnp.bfloat16


def nt(a, b):
    return lax.dot_general(a, b, (((1,), (1,)), ((), ())), preferred_element_type=F32)


def tn(a, b):
    return lax.dot_general(a, b, (((0,), (0,)), ((), ())), preferred_element_type=F32)


def kernel(
    heads,
    q_ref, k_ref, v_ref, slot_hbm, doc_hbm, out_ref,
    slot_ref, doc_ref, qg, kvg, bias, half_o, half_stat, op, orecv, zs, zr_buf, out_buf,
    tab_sem, loc_sem, zkv_s, zkv_r, zq_s, zq_r, kv_s, kv_r, q_s, q_r, c_s, c_r, o_s, o_r, zo_s, zo_r, out_sem,
):
    outer = lax.axis_index("outer")
    inner = lax.axis_index("inner")
    z, c = outer // 2, outer % 2
    x, y = inner // NX, inner % NX
    za = z + 1 - 2 * (z % 2)
    zb = 3 - z
    dev_c = {"outer": z * 2 + 1 - c, "inner": inner}
    first_heads = (heads + 1) // 2
    groups = (0, 1)
    of = (pl.ds(0, first_heads), pl.ds(first_heads, heads - first_heads))

    def pick(g, even, odd):
        return even + g * (odd - even)

    def group_of(h):
        return h // first_heads

    def plane_q(g):
        return {"outer": pick(g, za, zb) * 2 + c, "inner": inner}

    def plane_kv(g):
        return {"outer": pick(g, zb, za) * 2 + c, "inner": inner}

    def along_x(j):
        return lax.rem(x + j, NX) * NX + y

    def along_y(j):
        return x * NX + lax.rem(y + j, NX)

    def ring_q(g, j):
        return {"outer": outer, "inner": pick(g, along_x(j), along_y(j))}

    def ring_kv(g, j):
        return {"outer": outer, "inner": pick(g, along_y(j), along_x(j))}

    def at_q(g, j=0):
        return lax.rem(pick(g, x, y) + j, NX)

    def at_kv(g, j=0):
        return lax.rem(pick(g, y, x) + j, NX)

    tables = (
        pltpu.make_async_copy(slot_hbm, slot_ref, tab_sem.at[0]),
        pltpu.make_async_copy(doc_hbm, doc_ref, tab_sem.at[1]),
    )

    def local(h):
        at = pl.ds(h * D, D)
        g = group_of(h)
        return (
            pltpu.make_async_copy(q_ref.at[:, at], qg.at[at_q(g), 0, h], loc_sem.at[2, h]),
            pltpu.make_async_copy(k_ref.at[:, at], kvg.at[0, 0, 0, at_kv(g), h], loc_sem.at[0, h]),
            pltpu.make_async_copy(v_ref.at[:, at], kvg.at[1, 0, 0, at_kv(g), h], loc_sem.at[1, h]),
        )

    for h in range(heads):
        for copy in local(h):
            copy.start()
    for copy in tables:
        copy.start()

    barrier = pltpu.get_barrier_semaphore()
    partners = [plane_q(0), plane_kv(0), dev_c]
    partners += [ring_q(0, j) for j in (1, 2, 3)] + [ring_kv(0, j) for j in (1, 2, 3)]
    for dev in partners:
        pl.semaphore_signal(barrier, inc=1, device_id=dev, device_id_type=MESH)
    pl.semaphore_wait(barrier, len(partners))

    def remote(src, dst, send, recv, dev):
        return pltpu.make_async_remote_copy(
            src_ref=src, dst_ref=dst, send_sem=send, recv_sem=recv, device_id=dev, device_id_type=MESH
        )

    def z_kv(g):
        here = at_kv(g)
        return remote(
            kvg.at[:, 0, 0, here, of[g]], kvg.at[:, 0, 1, here, of[g]], zkv_s, zkv_r.at[g], plane_kv(g)
        )

    def z_q(g):
        here = at_q(g)
        return remote(qg.at[here, 0, of[g]], qg.at[here, 1, of[g]], zq_s, zq_r.at[g], plane_q(g))

    def r_kv(g, zr, j):
        block = kvg.at[:, 0, zr, at_kv(g), of[g]]
        return remote(block, block, kv_s, kv_r.at[g, zr], ring_kv(g, j))

    def r_q(g, zr, j):
        block = qg.at[at_q(g), zr, of[g]]
        return remote(block, block, q_s, q_r.at[g], ring_q(g, j))

    def c_kv(g, zr):
        return remote(
            kvg.at[:, 0, zr, :, of[g]], kvg.at[:, 1, zr, :, of[g]], c_s, c_r.at[g, zr], dev_c
        )

    def ring_o(h, zr, j):
        g = group_of(h)
        return remote(
            op.at[zr, h, at_q(g, j)], orecv.at[zr, h, j - 1], o_s, o_r.at[zr, h], ring_q(g, j)
        )

    def z_o(h):
        return remote(zs.at[h], zr_buf.at[h], zo_s, zo_r.at[h], plane_q(group_of(h)))

    def take(ref, sem):
        pltpu.make_async_copy(ref, ref, sem).wait()

    def out_copy(h):
        return pltpu.make_async_copy(
            out_buf.at[h], out_ref.at[:, pl.ds(pl.multiple_of(h * D, D), D)], out_sem
        )

    for h in range(heads):
        for copy in local(h):
            copy.wait()
    for g in groups:
        z_q(g).start()
        z_kv(g).start()
    for j in (1, 3, 2):
        for g in groups:
            r_kv(g, 0, j).start()
            r_q(g, 0, j).start()
    for copy in tables:
        copy.wait()

    ends = [doc_ref[0]]
    for n in range(1, doc_ref.shape[0]):
        ends.append(ends[-1] + doc_ref[n])

    def doc_start(slot):
        start = jnp.int32(0)
        for end in ends:
            start = jnp.where(slot >= end, end, start)
        return start

    lane = lax.broadcasted_iota(jnp.int32, (8, NQ), 1)
    down = lax.broadcasted_iota(jnp.int32, (8, NQ), 0)
    part = lane // BLK

    def build_mask(g):
        q_pos = jnp.zeros((8, NQ), jnp.int32)
        q_low = jnp.zeros((8, NQ), jnp.int32)
        for t in range(NQ // BLK):
            zt, half, rt = t // 8, (t // 4) % 2, t % 4
            zq = z if zt == 0 else (zb if g else za)
            iq = x * NX + rt if g else rt * NX + y
            slot = slot_ref[2 * ((zq * 2 + c) * 16 + iq) + half]
            hit = part == t
            q_pos = jnp.where(hit, slot * BLK, q_pos)
            q_low = jnp.where(hit, doc_start(slot) * BLK, q_low)
        q_pos = q_pos + lane % BLK

        def mask(t, carry):
            ct, zt, rt, half = t // 16, (t // 8) % 2, (t // 2) % 4, t % 2
            zk = z + zt * ((za if g else zb) - z)
            ck = c + ct * (1 - 2 * c)
            ik = rt * NX + y if g else x * NX + rt
            slot = slot_ref[2 * ((zk * 2 + ck) * 16 + ik) + half]
            for row in range(0, BLK, 8):
                k_pos = down + (slot * BLK + row)
                seen = (k_pos <= q_pos) & (k_pos >= q_low)
                at = (zt * 2 + half) * KT + (ct * NX + rt) * BLK + row
                term = jnp.where(seen, 0.0, HIDE)
                for tile in (0, 1):
                    bias[g, tile, pl.ds(pl.multiple_of(at, 8), 8), :] = term[:, tile * QT : (tile + 1) * QT]
            return carry

        lax.fori_loop(0, NK // BLK, mask, 0)

    def swap_cores(zr):
        for g in (1, 0):
            take(kvg.at[:, 0, zr, pl.ds(0, NX - 1), of[g]], kv_r.at[g, zr])
            c_kv(g, zr).start()

    def swap_half(a):
        return pltpu.roll(a, R, axis=1)

    quarter = lax.broadcasted_iota(jnp.int32, (1, D), 1) // BLK

    def gather_lanes(pieces, n):
        moved = [pltpu.roll(p, (k - n) % 4 * BLK, axis=1) if k != n else p for k, p in enumerate(pieces)]
        return jnp.where(
            quarter < 2, jnp.where(quarter == 0, moved[0], moved[1]), jnp.where(quarter == 2, moved[2], moved[3])
        )

    def attend(units, zr):
        half = QT // 2
        scores = []
        for h, tile in units:
            low_keys = kvg[0, :, zr, :, h, 0:BLK, :].reshape(KT, D)
            high_keys = kvg[0, :, zr, :, h, BLK:R, :].reshape(KT, D)
            low_rows = qg[:, tile, h, 0:BLK, :].reshape(half, D)
            high_rows = qg[:, tile, h, BLK:R, :].reshape(half, D)
            g, first = group_of(h), zr * 2 * KT
            rows = jnp.concatenate([low_rows, high_rows], axis=0)
            wide = nt(low_keys, rows) * SCALE2 + bias[g, tile, first : first + KT, :]
            tall = nt(high_keys, high_rows) * SCALE2 + bias[g, tile, first + KT : first + 2 * KT, half:QT]
            scores.append((wide, tall))
        tops = []
        for (h, tile), (wide, tall) in zip(units, scores):
            top = jnp.max(wide, axis=0, keepdims=True)
            low_top, high_top = top[:, 0:half], jnp.maximum(top[:, half:QT], jnp.max(tall, axis=0, keepdims=True))
            top = jnp.concatenate([low_top, high_top], axis=1)
            top = jnp.maximum(top, FLOOR).astype(BF16).astype(F32)
            if zr:
                top = jnp.maximum(top, half_stat[h, tile, 0:1, :])
            tops.append(top)
        results = []
        for (h, tile), (wide, tall), top in zip(units, scores, tops):
            wide = jnp.exp2(wide - top)
            tall = jnp.exp2(tall - top[:, half:QT])
            total = jnp.sum(wide, axis=0, keepdims=True)
            total = (total[:, 0:half], total[:, half:QT] + jnp.sum(tall, axis=0, keepdims=True))
            low_values = kvg[1, :, zr, :, h, 0:BLK, :].reshape(KT, D)
            high_values = kvg[1, :, zr, :, h, BLK:R, :].reshape(KT, D)
            result = tn(low_values, wide.astype(BF16))
            high_result = result[:, half:QT] + tn(high_values, tall.astype(BF16))
            results.append((total, (result[:, 0:half], high_result)))
        row = lax.broadcasted_iota(jnp.int32, (STAT, half), 0)
        for (h, tile), top, (total, result) in zip(units, tops, results):
            sides, stats = [], []
            for side in (0, 1):
                span = slice(side * half, (side + 1) * half)
                m, l, o = top[:, span], total[side], result[side]
                if not zr:
                    half_stat[h, tile, 0:1, span] = m
                    half_stat[h, tile, 1:2, span] = l
                    half_o[h, tile, :, span] = o
                    continue
                shrink = jnp.exp2(half_stat[h, tile, 0:1, span] - m)
                l = l + half_stat[h, tile, 1:2, span] * shrink
                sides.append(o + half_o[h, tile, :, span] * shrink)
                l_hi = l.astype(BF16).astype(F32)
                stats.append(jnp.where(row == 0, m, jnp.where(row == 1, l_hi, l - l_hi)))
            if not zr:
                continue
            pieces = (sides[0][0:R], sides[1][0:R], sides[0][R:D], sides[1][R:D])
            for n in range(NX):
                op[tile, h, n, 0:R, :] = gather_lanes(pieces, n).astype(BF16)
                op[tile, h, n, R : R + STAT, :] = gather_lanes(stats * 2, n).astype(BF16)

    def unstat(block):
        stat = block.astype(F32)
        return stat[0:1], stat[1:2] + stat[2:3]

    def merge_ring(h, zr):
        take(orecv.at[zr, h], o_r.at[zr, h])
        here = at_q(group_of(h))
        parts = [(op[zr, h, here, 0:R, :], unstat(op[zr, h, here, R : R + STAT, :]))]
        for j in (1, 2, 3):
            parts.append((orecv[zr, h, j - 1, 0:R, :], unstat(orecv[zr, h, j - 1, R : R + STAT, :])))
        top = functools.reduce(jnp.maximum, [p[1][0] for p in parts])
        total = jnp.zeros((1, D), F32)
        result = jnp.zeros((R, D), F32)
        for block, (m, l) in parts:
            w = jnp.exp2(m - top)
            total = total + w * l
            result = result + block.astype(F32) * w
        return result, top, total

    def merge_far(h):
        result, top, total = merge_ring(h, 1)
        total_hi = total.astype(BF16).astype(F32)
        row = lax.broadcasted_iota(jnp.int32, (STAT, D), 0)
        zs[h, 0:R, :] = result.astype(BF16)
        zs[h, R : R + STAT, :] = jnp.where(
            row == 0, top, jnp.where(row == 1, total_hi, total - total_hi)
        ).astype(BF16)
        z_o(h).start()

    def finish(h):
        result, m_own, l_own = merge_ring(h, 0)
        z_o(h).wait_recv()
        m_far, l_far = unstat(zr_buf[h, R : R + STAT, :])
        top = jnp.maximum(m_far, m_own)
        w_far, w_own = jnp.exp2(m_far - top), jnp.exp2(m_own - top)
        total = w_far * l_far + w_own * l_own
        w_far, w_own = w_far / total, w_own / total
        packed = result * w_own + zr_buf[h, 0:R, :].astype(F32) * w_far
        tall = jnp.concatenate([packed, swap_half(packed)], axis=0)
        out_buf[h] = tall.T[0:R].astype(BF16)
        out_copy(h).start()

    build_mask(0)
    build_mask(1)
    swap_cores(0)
    for g in groups:
        z_q(g).wait_recv()
        for j in (1, 3, 2):
            r_q(g, 1, j).start()
    for g in (1, 0):
        z_kv(g).wait_recv()
        for j in (1, 3, 2):
            r_kv(g, 1, j).start()
    for g in groups:
        take(qg.at[pl.ds(0, NX - 1), :, of[g]], q_r.at[g])
        c_kv(g, 0).wait_recv()

    def early(i, carry):
        attend([(i, 1), (i, 0)], 0)
        return carry

    lax.fori_loop(0, heads, early, 0)
    swap_cores(1)
    for g in (1, 0):
        c_kv(g, 1).wait_recv()

    def head_of(unit):
        return lax.rem(unit * first_heads, heads)

    def late(i, carry):
        @pl.when(i < heads)
        def _():
            units = (2 * i, 2 * i + 1)
            works = [(head_of(unit), jnp.where(unit < heads, 1, 0)) for unit in units]
            attend(works, 1)
            for h, tile in works:
                for j in (1, 3, 2):
                    ring_o(h, tile, j).start()

        for k in (0, 1):
            unit = 2 * (i - 2) + k

            @pl.when((unit >= 0) & (unit < heads))
            def _():
                merge_far(head_of(unit))

            @pl.when(unit >= heads)
            def _():
                finish(head_of(unit))

        return carry

    lax.fori_loop(0, heads + 2, late, 0)

    take(kvg.at[:, 0, 0, 0], zkv_s)
    take(qg.at[0, 0], zq_s)
    take(kvg.at[:, 0, :, pl.ds(0, NX - 1)], kv_s)
    take(qg.at[pl.ds(0, NX - 1)], q_s)
    take(kvg.at[:, 0], c_s)
    take(orecv, o_s)
    take(zs, zo_s)
    take(out_buf, out_sem)


def per_device(queries, keys, values, slot_blocks, doc_blocks):
    width = queries.shape[1]
    heads = width // D
    dma = pltpu.SemaphoreType.DMA
    anywhere = pl.BlockSpec(memory_space=pltpu.HBM)
    return pl.pallas_call(
        functools.partial(kernel, heads),
        out_shape=jax.ShapeDtypeStruct(queries.shape, BF16),
        in_specs=[anywhere] * 5,
        out_specs=anywhere,
        scratch_shapes=[
            pltpu.SMEM(slot_blocks.shape, jnp.int32),
            pltpu.SMEM(doc_blocks.shape, jnp.int32),
            pltpu.VMEM((NX, NZ, heads, R, D), BF16),
            pltpu.VMEM((2, NC, NZ, NX, heads, R, D), BF16),
            pltpu.VMEM((2, NZ, NK, QT), F32),
            pltpu.VMEM((heads, NZ, D, QT), F32),
            pltpu.VMEM((heads, NZ, 8, QT), F32),
            pltpu.VMEM((NZ, heads, NX, R + STAT, D), BF16),
            pltpu.VMEM((NZ, heads, NX - 1, R + STAT, D), BF16),
            pltpu.VMEM((heads, R + STAT, D), BF16),
            pltpu.VMEM((heads, R + STAT, D), BF16),
            pltpu.VMEM((heads, R, D), BF16),
            dma((2,)),
            dma((3, heads)),
            dma, dma((2,)), dma, dma((2,)),
            dma, dma((2, 2)), dma, dma((2,)),
            dma, dma((2, 2)),
            dma, dma((2, heads)),
            dma, dma((heads,)), dma,
        ],
        compiler_params=pltpu.CompilerParams(
            collective_id=0, has_side_effects=True, vmem_limit_bytes=64 * 1024 * 1024
        ),
        cost_estimate=pl.CostEstimate(
            flops=4 * heads * NQ * NK * D, bytes_accessed=4 * queries.size * 2, transcendentals=heads * NQ * NK
        ),
    )(queries, keys, values, slot_blocks, doc_blocks)


def solution(mesh):
    rows = P(("outer", "inner"), "head")
    return jax.shard_map(
        per_device,
        mesh=mesh,
        in_specs=(rows, rows, rows, P(), P()),
        out_specs=rows,
        check_vma=False,
    )
```

profile of v0, /device:TPU:1, one launch (start us, length us, event | category | flops | bytes accessed | tf_op | source)
XLA Modules:
  0.0 53.7 jit_solution(15764284766120674306)
XLA Ops:
  0.0 52.1 %shard_map.55 = bf16[64,640]{1,0:T(8,128)(2,1)} custom-call(bf16[64,640]{1,0:T(8,128)(2,1)} %q_ref.1, bf16[64,640]{1,0:T(8,128)(2,1)} %k_ref.1, bf16[64,640]{1,0:T(8,128)(2,1)} %v_ref.1, s32[256]{0:T(256)} %slot_hbm.1, s32[4]{0:T(128)} %doc_hbm.1), custom_call_target="tpu_custom_call" | custom-call | flops 1342177280 | bytes 327680 | tf_op jit(solution)/shard_map/pallas_call | solution.py:395
  52.2 1.5 %copy.7 = bf16[64,640]{1,0:T(8,128)(2,1)} copy(bf16[64,640]{1,0:T(8,128)(2,1)} %shard_map.55) | data formatting | bytes 163840
where the time goes:
time: 53.8 us; the launch traced here: 53.7 us
  Pallas kernels  52.1 us (97%)
  local copies, waits for them, and re-layouts  1.53 us (3%)
    pallas_call x1, Pallas kernels, per_device(): pl.pallas_call(functools.partial(kernel, heads), out_shape=jax.ShapeDtype...  52.1 us
    unnamed x1, local copies, waits for them, and re-layouts  1.53 us

commit v1 on v0

--- a/solution.py
+++ b/solution.py
@@ -180,9 +180,10 @@
     lane = lax.broadcasted_iota(jnp.int32, (8, NQ), 1)
     down = lax.broadcasted_iota(jnp.int32, (8, NQ), 0)
     part = lane // BLK
+    diagonal = [jnp.where(down + row <= lane % BLK, 0.0, HIDE) for row in range(0, BLK, 8)]
 
     def build_mask(g):
-        q_pos = jnp.zeros((8, NQ), jnp.int32)
+        q_slot = jnp.zeros((8, NQ), jnp.int32)
         q_low = jnp.zeros((8, NQ), jnp.int32)
         for t in range(NQ // BLK):
             zt, half, rt = t // 8, (t // 4) % 2, t % 4
@@ -190,26 +191,26 @@
             iq = x * NX + rt if g else rt * NX + y
             slot = slot_ref[2 * ((zq * 2 + c) * 16 + iq) + half]
             hit = part == t
-            q_pos = jnp.where(hit, slot * BLK, q_pos)
-            q_low = jnp.where(hit, doc_start(slot) * BLK, q_low)
-        q_pos = q_pos + lane % BLK
+            q_slot = jnp.where(hit, slot, q_slot)
+            q_low = jnp.where(hit, doc_start(slot), q_low)
 
         def mask(t, carry):
-            ct, zt, rt, half = t // 16, (t // 8) % 2, (t // 2) % 4, t % 2
+            ct, zt, half = t // 4, (t // 2) % 2, t % 2
             zk = z + zt * ((za if g else zb) - z)
             ck = c + ct * (1 - 2 * c)
-            ik = rt * NX + y if g else x * NX + rt
-            slot = slot_ref[2 * ((zk * 2 + ck) * 16 + ik) + half]
-            for row in range(0, BLK, 8):
-                k_pos = down + (slot * BLK + row)
-                seen = (k_pos <= q_pos) & (k_pos >= q_low)
-                at = (zt * 2 + half) * KT + (ct * NX + rt) * BLK + row
-                term = jnp.where(seen, 0.0, HIDE)
-                for tile in (0, 1):
-                    bias[g, tile, pl.ds(pl.multiple_of(at, 8), 8), :] = term[:, tile * QT : (tile + 1) * QT]
+            for rt in range(NX):
+                ik = rt * NX + y if g else x * NX + rt
+                slot = slot_ref[2 * ((zk * 2 + ck) * 16 + ik) + half]
+                before = jnp.where((slot < q_slot) & (slot >= q_low), 0.0, HIDE)
+                same = q_slot == slot
+                for row in range(0, BLK, 8):
+                    at = (zt * 2 + half) * KT + (ct * NX + rt) * BLK + row
+                    term = jnp.where(same, diagonal[row // 8], before)
+                    for tile in (0, 1):
+                        bias[g, tile, pl.ds(pl.multiple_of(at, 8), 8), :] = term[:, tile * QT : (tile + 1) * QT]
             return carry
 
-        lax.fori_loop(0, NK // BLK, mask, 0)
+        lax.fori_loop(0, NC * NZ * 2, mask, 0)
 
     def swap_cores(zr):
         for g in (1, 0):

time: 53.8 us -> 53.8 us (level)
  no operation moved by 1% of the time
where the time goes in v1:
time: 53.8 us; the launch traced here: 53.7 us
  Pallas kernels  52.1 us (97%)
  local copies, waits for them, and re-layouts  1.53 us (3%)
    pallas_call x1, Pallas kernels, per_device(): pl.pallas_call(functools.partial(kernel, heads), out_shape=jax.ShapeDtype...  52.1 us
    unnamed x1, local copies, waits for them, and re-layouts  1.53 us

profile of v1, /device:TPU:1, one launch (start us, length us, event | category | flops | bytes accessed | tf_op | source)
XLA Modules:
  0.0 53.7 jit_solution(805108927518561478)
XLA Ops:
  0.0 52.1 %shard_map.55 = bf16[64,640]{1,0:T(8,128)(2,1)} custom-call(bf16[64,640]{1,0:T(8,128)(2,1)} %q_ref.1, bf16[64,640]{1,0:T(8,128)(2,1)} %k_ref.1, bf16[64,640]{1,0:T(8,128)(2,1)} %v_ref.1, s32[256]{0:T(256)} %slot_hbm.1, s32[4]{0:T(128)} %doc_hbm.1), custom_call_target="tpu_custom_call" | custom-call | flops 1342177280 | bytes 327680 | tf_op jit(solution)/shard_map/pallas_call | solution.py:396
  52.1 1.5 %copy.7 = bf16[64,640]{1,0:T(8,128)(2,1)} copy(bf16[64,640]{1,0:T(8,128)(2,1)} %shard_map.55) | data formatting | bytes 163840

commit v2 on v1

--- a/solution.py
+++ b/solution.py
@@ -117,7 +117,7 @@
     def z_kv(g):
         here = at_kv(g)
         return remote(
-            kvg.at[:, 0, 0, here, of[g]], kvg.at[:, 0, 1, here, of[g]], zkv_s, zkv_r.at[g], plane_kv(g)
+            kvg.at[:, 0, 0, here, of[g]], kvg.at[:, 0, 1, here, of[g]], zkv_s.at[g], zkv_r.at[g], plane_kv(g)
         )
 
     def z_q(g):
@@ -130,7 +130,7 @@
 
     def r_q(g, zr, j):
         block = qg.at[at_q(g), zr, of[g]]
-        return remote(block, block, q_s, q_r.at[g], ring_q(g, j))
+        return remote(block, block, q_s, q_r.at[g, zr], ring_q(g, j))
 
     def c_kv(g, zr):
         return remote(
@@ -158,11 +158,12 @@
         for copy in local(h):
             copy.wait()
     for g in groups:
-        z_q(g).start()
         z_kv(g).start()
     for j in (1, 3, 2):
         for g in groups:
             r_kv(g, 0, j).start()
+    for j in (1, 3, 2):
+        for g in groups:
             r_q(g, 0, j).start()
     for copy in tables:
         copy.wait()
@@ -330,22 +331,27 @@
     build_mask(1)
     swap_cores(0)
     for g in groups:
+        z_kv(g).wait_send()
+        z_q(g).start()
+    for g in groups:
+        z_kv(g).wait_recv()
+        for j in (1, 3, 2):
+            r_kv(g, 1, j).start()
+
+    def early(tile):
+        for g in groups:
+            take(qg.at[pl.ds(0, NX - 1), tile, of[g]], q_r.at[g, tile])
+        for h in range(0, heads, 2):
+            attend([(n, tile) for n in range(h, min(h + 2, heads))], 0)
+
+    for g in groups:
+        c_kv(g, 0).wait_recv()
+    early(0)
+    for g in groups:
         z_q(g).wait_recv()
         for j in (1, 3, 2):
             r_q(g, 1, j).start()
-    for g in (1, 0):
-        z_kv(g).wait_recv()
-        for j in (1, 3, 2):
-            r_kv(g, 1, j).start()
-    for g in groups:
-        take(qg.at[pl.ds(0, NX - 1), :, of[g]], q_r.at[g])
-        c_kv(g, 0).wait_recv()
-
-    def early(i, carry):
-        attend([(i, 1), (i, 0)], 0)
-        return carry
-
-    lax.fori_loop(0, heads, early, 0)
+    early(1)
     swap_cores(1)
     for g in (1, 0):
         c_kv(g, 1).wait_recv()
@@ -378,7 +384,6 @@
 
     lax.fori_loop(0, heads + 2, late, 0)
 
-    take(kvg.at[:, 0, 0, 0], zkv_s)
     take(qg.at[0, 0], zq_s)
     take(kvg.at[:, 0, :, pl.ds(0, NX - 1)], kv_s)
     take(qg.at[pl.ds(0, NX - 1)], q_s)
@@ -413,8 +418,8 @@
             pltpu.VMEM((heads, R, D), BF16),
             dma((2,)),
             dma((3, heads)),
-            dma, dma((2,)), dma, dma((2,)),
-            dma, dma((2, 2)), dma, dma((2,)),
+            dma((2,)), dma((2,)), dma, dma((2,)),
+            dma, dma((2, 2)), dma, dma((2, 2)),
             dma, dma((2, 2)),
             dma, dma((2, heads)),
             dma, dma((heads,)), dma,

time: 53.8 us -> 52.8 us (0.981)
  Pallas kernels: 52.1 us -> 51.1 us
    pallas_call x1, Pallas kernels: 52.1 us -> 51.1 us  [per_device(): pl.pallas_call(functools.partial(kernel, heads), out_shape=jax.ShapeDtype...]
where the time goes in v2:
time: 52.8 us; the launch traced here: 52.7 us
  Pallas kernels  51.1 us (97%)
  local copies, waits for them, and re-layouts  1.53 us (3%)
    pallas_call x1, Pallas kernels, per_device(): pl.pallas_call(functools.partial(kernel, heads), out_shape=jax.ShapeDtype...  51.1 us
    unnamed x1, local copies, waits for them, and re-layouts  1.53 us

profile of v2, /device:TPU:1, one launch (start us, length us, event | category | flops | bytes accessed | tf_op | source)
XLA Modules:
  0.0 52.7 jit_solution(8051505943800332213)
XLA Ops:
  0.0 51.1 %shard_map.55 = bf16[64,640]{1,0:T(8,128)(2,1)} custom-call(bf16[64,640]{1,0:T(8,128)(2,1)} %q_ref.1, bf16[64,640]{1,0:T(8,128)(2,1)} %k_ref.1, bf16[64,640]{1,0:T(8,128)(2,1)} %v_ref.1, s32[256]{0:T(256)} %slot_hbm.1, s32[4]{0:T(128)} %doc_hbm.1), custom_call_target="tpu_custom_call" | custom-call | flops 1342177280 | bytes 327680 | tf_op jit(solution)/shard_map/pallas_call | solution.py:401
  51.1 1.5 %copy.7 = bf16[64,640]{1,0:T(8,128)(2,1)} copy(bf16[64,640]{1,0:T(8,128)(2,1)} %shard_map.55) | data formatting | bytes 163840

commit v3 on v2

--- a/solution.py
+++ b/solution.py
@@ -52,6 +52,8 @@
     groups = (0, 1)
     of = (pl.ds(0, first_heads), pl.ds(first_heads, heads - first_heads))
 
+    pieces = ((0, first_heads - 1, 1), (0, 0, first_heads - 1), (1, first_heads, heads - first_heads))
+
     def pick(g, even, odd):
         return even + g * (odd - even)
 
@@ -114,28 +116,29 @@
             src_ref=src, dst_ref=dst, send_sem=send, recv_sem=recv, device_id=dev, device_id_type=MESH
         )
 
-    def z_kv(g):
+    def z_kv(p):
+        g, first, count = pieces[p]
+        at = pl.ds(first, count)
         here = at_kv(g)
-        return remote(
-            kvg.at[:, 0, 0, here, of[g]], kvg.at[:, 0, 1, here, of[g]], zkv_s.at[g], zkv_r.at[g], plane_kv(g)
-        )
+        return remote(kvg.at[:, 0, 0, here, at], kvg.at[:, 0, 1, here, at], zkv_s.at[p], zkv_r.at[p], plane_kv(g))
 
     def z_q(g):
         here = at_q(g)
         return remote(qg.at[here, 0, of[g]], qg.at[here, 1, of[g]], zq_s, zq_r.at[g], plane_q(g))
 
-    def r_kv(g, zr, j):
-        block = kvg.at[:, 0, zr, at_kv(g), of[g]]
-        return remote(block, block, kv_s, kv_r.at[g, zr], ring_kv(g, j))
+    def r_kv(p, zr, j):
+        g, first, count = pieces[p]
+        block = kvg.at[:, 0, zr, at_kv(g), pl.ds(first, count)]
+        return remote(block, block, kv_s, kv_r.at[p, zr], ring_kv(g, j))
 
     def r_q(g, zr, j):
         block = qg.at[at_q(g), zr, of[g]]
         return remote(block, block, q_s, q_r.at[g, zr], ring_q(g, j))
 
-    def c_kv(g, zr):
-        return remote(
-            kvg.at[:, 0, zr, :, of[g]], kvg.at[:, 1, zr, :, of[g]], c_s, c_r.at[g, zr], dev_c
-        )
+    def c_kv(p, zr):
+        g, first, count = pieces[p]
+        at = pl.ds(first, count)
+        return remote(kvg.at[:, 0, zr, :, at], kvg.at[:, 1, zr, :, at], c_s, c_r.at[p, zr], dev_c)
 
     def ring_o(h, zr, j):
         g = group_of(h)
@@ -157,11 +160,11 @@
     for h in range(heads):
         for copy in local(h):
             copy.wait()
-    for g in groups:
-        z_kv(g).start()
-    for j in (1, 3, 2):
-        for g in groups:
-            r_kv(g, 0, j).start()
+    for p in (0, 2, 1):
+        z_kv(p).start()
+    for p in (0, 2, 1):
+        for j in (1, 3, 2):
+            r_kv(p, 0, j).start()
     for j in (1, 3, 2):
         for g in groups:
             r_q(g, 0, j).start()
@@ -214,9 +217,15 @@
         lax.fori_loop(0, NC * NZ * 2, mask, 0)
 
     def swap_cores(zr):
-        for g in (1, 0):
-            take(kvg.at[:, 0, zr, pl.ds(0, NX - 1), of[g]], kv_r.at[g, zr])
-            c_kv(g, zr).start()
+        for p in (0, 2, 1):
+            g, first, count = pieces[p]
+            take(kvg.at[:, 0, zr, pl.ds(0, NX - 1), pl.ds(first, count)], kv_r.at[p, zr])
+            c_kv(p, zr).start()
+
+    def spread_kv(p):
+        z_kv(p).wait_recv()
+        for j in (1, 3, 2):
+            r_kv(p, 1, j).start()
 
     def swap_half(a):
         return pltpu.roll(a, R, axis=1)
@@ -330,13 +339,14 @@
     build_mask(0)
     build_mask(1)
     swap_cores(0)
-    for g in groups:
-        z_kv(g).wait_send()
-        z_q(g).start()
-    for g in groups:
-        z_kv(g).wait_recv()
-        for j in (1, 3, 2):
-            r_kv(g, 1, j).start()
+    z_kv(2).wait_send()
+    z_q(0).start()
+    spread_kv(0)
+    spread_kv(2)
+    for p in (0, 1):
+        z_kv(p).wait_send()
+    z_q(1).start()
+    spread_kv(1)
 
     def early(tile):
         for g in groups:
@@ -344,8 +354,8 @@
         for h in range(0, heads, 2):
             attend([(n, tile) for n in range(h, min(h + 2, heads))], 0)
 
-    for g in groups:
-        c_kv(g, 0).wait_recv()
+    for p in (0, 1, 2):
+        c_kv(p, 0).wait_recv()
     early(0)
     for g in groups:
         z_q(g).wait_recv()
@@ -353,13 +363,17 @@
             r_q(g, 1, j).start()
     early(1)
     swap_cores(1)
-    for g in (1, 0):
-        c_kv(g, 1).wait_recv()
+    for p in (0, 2):
+        c_kv(p, 1).wait_recv()
 
     def head_of(unit):
-        return lax.rem(unit * first_heads, heads)
+        return lax.rem(unit + first_heads - 1, heads)
 
     def late(i, carry):
+        @pl.when(i == 1)
+        def _():
+            c_kv(1, 1).wait_recv()
+
         @pl.when(i < heads)
         def _():
             units = (2 * i, 2 * i + 1)
@@ -418,9 +432,9 @@
             pltpu.VMEM((heads, R, D), BF16),
             dma((2,)),
             dma((3, heads)),
-            dma((2,)), dma((2,)), dma, dma((2,)),
-            dma, dma((2, 2)), dma, dma((2, 2)),
-            dma, dma((2, 2)),
+            dma((3,)), dma((3,)), dma, dma((2,)),
+            dma, dma((3, 2)), dma, dma((2, 2)),
+            dma, dma((3, 2)),
             dma, dma((2, heads)),
             dma, dma((heads,)), dma,
         ],

time: 52.8 us -> 53.5 us (1.013)
  Pallas kernels: 51.1 us -> 51.8 us
    pallas_call x1, Pallas kernels: 51.1 us -> 51.8 us  [per_device(): pl.pallas_call(functools.partial(kernel, heads), out_shape=jax.ShapeDtype...]
where the time goes in v3:
time: 53.5 us; the launch traced here: 53.3 us
  Pallas kernels  51.8 us (97%)
  local copies, waits for them, and re-layouts  1.53 us (3%)
    pallas_call x1, Pallas kernels, per_device(): pl.pallas_call(functools.partial(kernel, heads), out_shape=jax.ShapeDtype...  51.8 us
    unnamed x1, local copies, waits for them, and re-layouts  1.53 us

profile of v3, /device:TPU:1, one launch (start us, length us, event | category | flops | bytes accessed | tf_op | source)
XLA Modules:
  0.0 53.3 jit_solution(12203875009110841866)
XLA Ops:
  0.0 51.8 %shard_map.55 = bf16[64,640]{1,0:T(8,128)(2,1)} custom-call(bf16[64,640]{1,0:T(8,128)(2,1)} %q_ref.1, bf16[64,640]{1,0:T(8,128)(2,1)} %k_ref.1, bf16[64,640]{1,0:T(8,128)(2,1)} %v_ref.1, s32[256]{0:T(256)} %slot_hbm.1, s32[4]{0:T(128)} %doc_hbm.1), custom_call_target="tpu_custom_call" | custom-call | flops 1342177280 | bytes 327680 | tf_op jit(solution)/shard_map/pallas_call | solution.py:415
  51.8 1.5 %copy.7 = bf16[64,640]{1,0:T(8,128)(2,1)} copy(bf16[64,640]{1,0:T(8,128)(2,1)} %shard_map.55) | data formatting | bytes 163840

commit v4 on v2

--- a/solution.py
+++ b/solution.py
@@ -330,10 +330,10 @@
     build_mask(0)
     build_mask(1)
     swap_cores(0)
-    for g in groups:
+    for g in (1, 0):
         z_kv(g).wait_send()
-        z_q(g).start()
-    for g in groups:
+        z_q(1 - g).start()
+    for g in (1, 0):
         z_kv(g).wait_recv()
         for j in (1, 3, 2):
             r_kv(g, 1, j).start()
@@ -353,13 +353,16 @@
             r_q(g, 1, j).start()
     early(1)
     swap_cores(1)
-    for g in (1, 0):
-        c_kv(g, 1).wait_recv()
+    c_kv(1, 1).wait_recv()
 
     def head_of(unit):
-        return lax.rem(unit * first_heads, heads)
+        return lax.rem(unit + jnp.where(unit < heads, first_heads, 0), heads)
 
     def late(i, carry):
+        @pl.when(i == 1)
+        def _():
+            c_kv(0, 1).wait_recv()
+
         @pl.when(i < heads)
         def _():
             units = (2 * i, 2 * i + 1)

time: 52.8 us -> 53.9 us (1.021)
  Pallas kernels: 51.1 us -> 52.2 us
    pallas_call x1, Pallas kernels: 51.1 us -> 52.2 us  [per_device(): pl.pallas_call(functools.partial(kernel, heads), out_shape=jax.ShapeDtype...]
where the time goes in v4:
time: 53.9 us; the launch traced here: 53.7 us
  Pallas kernels  52.2 us (97%)
  local copies, waits for them, and re-layouts  1.53 us (3%)
    pallas_call x1, Pallas kernels, per_device(): pl.pallas_call(functools.partial(kernel, heads), out_shape=jax.ShapeDtype...  52.2 us
    unnamed x1, local copies, waits for them, and re-layouts  1.53 us

profile of v4, /device:TPU:1, one launch (start us, length us, event | category | flops | bytes accessed | tf_op | source)
XLA Modules:
  0.0 53.7 jit_solution(12965893537631435227)
XLA Ops:
  0.0 52.2 %shard_map.55 = bf16[64,640]{1,0:T(8,128)(2,1)} custom-call(bf16[64,640]{1,0:T(8,128)(2,1)} %q_ref.1, bf16[64,640]{1,0:T(8,128)(2,1)} %k_ref.1, bf16[64,640]{1,0:T(8,128)(2,1)} %v_ref.1, s32[256]{0:T(256)} %slot_hbm.1, s32[4]{0:T(128)} %doc_hbm.1), custom_call_target="tpu_custom_call" | custom-call | flops 1342177280 | bytes 327680 | tf_op jit(solution)/shard_map/pallas_call | solution.py:404
  52.2 1.5 %copy.7 = bf16[64,640]{1,0:T(8,128)(2,1)} copy(bf16[64,640]{1,0:T(8,128)(2,1)} %shard_map.55) | data formatting | bytes 163840

commit v5 on v2

--- a/solution.py
+++ b/solution.py
@@ -330,9 +330,9 @@
     build_mask(0)
     build_mask(1)
     swap_cores(0)
-    for g in groups:
+    for g in (1, 0):
         z_kv(g).wait_send()
-        z_q(g).start()
+        z_q(1 - g).start()
     for g in groups:
         z_kv(g).wait_recv()
         for j in (1, 3, 2):
@@ -370,7 +370,7 @@
                     ring_o(h, tile, j).start()
 
         for k in (0, 1):
-            unit = 2 * (i - 2) + k
+            unit = 2 * (i - 3) + k
 
             @pl.when((unit >= 0) & (unit < heads))
             def _():
@@ -382,7 +382,7 @@
 
         return carry
 
-    lax.fori_loop(0, heads + 2, late, 0)
+    lax.fori_loop(0, heads + 3, late, 0)
 
     take(qg.at[0, 0], zq_s)
     take(kvg.at[:, 0, :, pl.ds(0, NX - 1)], kv_s)

time: 52.8 us -> 53.4 us (1.011)
  Pallas kernels: 51.1 us -> 51.7 us
    pallas_call x1, Pallas kernels: 51.1 us -> 51.7 us  [per_device(): pl.pallas_call(functools.partial(kernel, heads), out_shape=jax.ShapeDtype...]
where the time goes in v5:
time: 53.4 us; the launch traced here: 53.2 us
  Pallas kernels  51.7 us (97%)
  local copies, waits for them, and re-layouts  1.53 us (3%)
    pallas_call x1, Pallas kernels, per_device(): pl.pallas_call(functools.partial(kernel, heads), out_shape=jax.ShapeDtype...  51.7 us
    unnamed x1, local copies, waits for them, and re-layouts  1.53 us

profile of v5, /device:TPU:1, one launch (start us, length us, event | category | flops | bytes accessed | tf_op | source)
XLA Modules:
  0.0 53.2 jit_solution(3277848202928754453)
XLA Ops:
  0.0 51.7 %shard_map.55 = bf16[64,640]{1,0:T(8,128)(2,1)} custom-call(bf16[64,640]{1,0:T(8,128)(2,1)} %q_ref.1, bf16[64,640]{1,0:T(8,128)(2,1)} %k_ref.1, bf16[64,640]{1,0:T(8,128)(2,1)} %v_ref.1, s32[256]{0:T(256)} %slot_hbm.1, s32[4]{0:T(128)} %doc_hbm.1), custom_call_target="tpu_custom_call" | custom-call | flops 1342177280 | bytes 327680 | tf_op jit(solution)/shard_map/pallas_call | solution.py:401
  51.7 1.5 %copy.7 = bf16[64,640]{1,0:T(8,128)(2,1)} copy(bf16[64,640]{1,0:T(8,128)(2,1)} %shard_map.55) | data formatting | bytes 163840

commit v6 on v2

--- a/solution.py
+++ b/solution.py
@@ -159,10 +159,10 @@
             copy.wait()
     for g in groups:
         z_kv(g).start()
-    for j in (1, 3, 2):
+    for j in (2, 1, 3):
         for g in groups:
             r_kv(g, 0, j).start()
-    for j in (1, 3, 2):
+    for j in (2, 1, 3):
         for g in groups:
             r_q(g, 0, j).start()
     for copy in tables:
@@ -335,7 +335,7 @@
         z_q(g).start()
     for g in groups:
         z_kv(g).wait_recv()
-        for j in (1, 3, 2):
+        for j in (2, 1, 3):
             r_kv(g, 1, j).start()
 
     def early(tile):
@@ -349,7 +349,7 @@
     early(0)
     for g in groups:
         z_q(g).wait_recv()
-        for j in (1, 3, 2):
+        for j in (2, 1, 3):
             r_q(g, 1, j).start()
     early(1)
     swap_cores(1)
@@ -366,7 +366,7 @@
             works = [(head_of(unit), jnp.where(unit < heads, 1, 0)) for unit in units]
             attend(works, 1)
             for h, tile in works:
-                for j in (1, 3, 2):
+                for j in (2, 1, 3):
                     ring_o(h, tile, j).start()
 
         for k in (0, 1):

time: 52.8 us -> 52.7 us (level)
  no operation moved by 1% of the time
where the time goes in v6:
time: 52.7 us; the launch traced here: 52.5 us
  Pallas kernels  51 us (97%)
  local copies, waits for them, and re-layouts  1.53 us (3%)
    pallas_call x1, Pallas kernels, per_device(): pl.pallas_call(functools.partial(kernel, heads), out_shape=jax.ShapeDtype...  51 us
    unnamed x1, local copies, waits for them, and re-layouts  1.53 us

profile of v6, /device:TPU:1, one launch (start us, length us, event | category | flops | bytes accessed | tf_op | source)
XLA Modules:
  0.0 52.5 jit_solution(13194939473420982198)
XLA Ops:
  0.0 51.0 %shard_map.55 = bf16[64,640]{1,0:T(8,128)(2,1)} custom-call(bf16[64,640]{1,0:T(8,128)(2,1)} %q_ref.1, bf16[64,640]{1,0:T(8,128)(2,1)} %k_ref.1, bf16[64,640]{1,0:T(8,128)(2,1)} %v_ref.1, s32[256]{0:T(256)} %slot_hbm.1, s32[4]{0:T(128)} %doc_hbm.1), custom_call_target="tpu_custom_call" | custom-call | flops 1342177280 | bytes 327680 | tf_op jit(solution)/shard_map/pallas_call | solution.py:401
  51.0 1.5 %copy.7 = bf16[64,640]{1,0:T(8,128)(2,1)} copy(bf16[64,640]{1,0:T(8,128)(2,1)} %shard_map.55) | data formatting | bytes 163840

commit v7 on v6

--- a/solution.py
+++ b/solution.py
@@ -330,9 +330,9 @@
     build_mask(0)
     build_mask(1)
     swap_cores(0)
-    for g in groups:
+    for g in (1, 0):
         z_kv(g).wait_send()
-        z_q(g).start()
+        z_q(1 - g).start()
     for g in groups:
         z_kv(g).wait_recv()
         for j in (2, 1, 3):

time: 52.7 us -> 52.7 us (level)
  no operation moved by 1% of the time
where the time goes in v7:
time: 52.7 us; the launch traced here: 52.5 us
  Pallas kernels  51 us (97%)
  local copies, waits for them, and re-layouts  1.53 us (3%)
    pallas_call x1, Pallas kernels, per_device(): pl.pallas_call(functools.partial(kernel, heads), out_shape=jax.ShapeDtype...  51 us
    unnamed x1, local copies, waits for them, and re-layouts  1.53 us

profile of v7, /device:TPU:1, one launch (start us, length us, event | category | flops | bytes accessed | tf_op | source)
XLA Modules:
  0.0 52.5 jit_solution(16599243953260515654)
XLA Ops:
  0.0 51.0 %shard_map.55 = bf16[64,640]{1,0:T(8,128)(2,1)} custom-call(bf16[64,640]{1,0:T(8,128)(2,1)} %q_ref.1, bf16[64,640]{1,0:T(8,128)(2,1)} %k_ref.1, bf16[64,640]{1,0:T(8,128)(2,1)} %v_ref.1, s32[256]{0:T(256)} %slot_hbm.1, s32[4]{0:T(128)} %doc_hbm.1), custom_call_target="tpu_custom_call" | custom-call | flops 1342177280 | bytes 327680 | tf_op jit(solution)/shard_map/pallas_call | solution.py:401
  51.0 1.5 %copy.7 = bf16[64,640]{1,0:T(8,128)(2,1)} copy(bf16[64,640]{1,0:T(8,128)(2,1)} %shard_map.55) | data formatting | bytes 163840
